TPU v7x, 128 devices: a whole 4x4x4 slice. The times are simulated.
128 devices in a mesh: dp: 64 (over z, y, x_hi, core), cent: 2 (over x_lo).
Axes of the slice: x: 4 (x_hi: 2, x_lo: 2; x = x_hi * 2 + x_lo), y: 4, z: 4, core: 2. Of those that a mesh axis runs over, the one named last changes fastest.
Arguments:
- vectors: float32 [131072, 768], P('dp'), may hold values from -24 to 24
- centroids: float32 [4096, 768], P('cent'), may hold values from -8 to 8
- head_index: int32 [2, 512], P('cent'), may hold values from 0 to 2047, as said below
- boundary_rows: int32 [64, 2, 512], P('dp', 'cent'), may hold values from 0 to 2047, as said below
- block_owner: int32 [64, 2, 4], P('dp', 'cent'), may hold values from 0 to 1, as said below
- block_live: int32 [64, 2, 4], P('dp', 'cent'), may hold values from 49 to 128
Outputs:
- new_centroids: float32 [2, 2048, 768], P('cent', 'dp')
- second_resid: bfloat16 [64, 2, 512, 768], P('dp', 'cent')
Inputs may be any that keep to these rules, and one draw needn't show every extreme that they name: `head_index`: each owner's row holds 512 distinct local indices of its 2048 centroids. `boundary_rows`: each sender lists 512 distinct rows of the 2048 vector rows of its dp index; slots past a block's live count are padding. `block_owner`: no owner appears more than 2 times among one sender's 4 blocks, and some owner appears exactly 2 times in every sender; in some dp index every sender gives one owner 2 blocks.
All inputs are finite; a program needn't handle non-finite values.
Results may differ from a plain program's by a relative error of at most 0.012.
Values may be sent and summed in bfloat16 or wider, within the bound.
A program may use at most 128 MiB of HBM per device.

v0:
```python
import jax
import jax.numpy as jnp
from jax import lax
from jax.sharding import PartitionSpec as P

MOSTB = 2


smoothing_divisor = 20.0


def match_rows(queries, head_rows, leading_length_power):
    query_f = queries.astype(jnp.float32)
    probe_length_power = jnp.sum(query_f * query_f, axis=1)
    pairwise_dots = lax.dot_general(
        queries, head_rows, (((1,), (1,)), ((), ())), preferred_element_type=jnp.float32
    )
    cluster_affinity = (
        2.0 * pairwise_dots - probe_length_power[:, None] - leading_length_power[None, :]
    ) / smoothing_divisor
    row_top = jnp.max(cluster_affinity, axis=1, keepdims=True)
    exponent = jnp.exp(cluster_affinity - row_top)
    weights = (exponent / jnp.sum(exponent, axis=1, keepdims=True)).astype(jnp.bfloat16)
    mixture = jnp.dot(weights, head_rows, preferred_element_type=jnp.float32)
    return (query_f - mixture).astype(jnp.bfloat16)


def per_device(vectors, centroids, head_index, boundary_rows, block_owner, block_live):
    width = vectors.shape[1]
    centre_count = centroids.shape[0]
    quantized = lax.optimization_barrier(vectors.astype(jnp.bfloat16))
    centre_q = lax.optimization_barrier(centroids.astype(jnp.bfloat16))
    quant_f = quantized.astype(jnp.float32)
    entry_length_power = jnp.sum(quant_f * quant_f, axis=1)
    centre_f = centre_q.astype(jnp.float32)
    centre_length_power = jnp.sum(centre_f * centre_f, axis=1)
    pairwise_dots = lax.dot_general(
        quantized, centre_q, (((1,), (1,)), ((), ())), preferred_element_type=jnp.float32
    )
    cluster_affinity = (
        2.0 * pairwise_dots - entry_length_power[:, None] - centre_length_power[None, :]
    ) / smoothing_divisor
    local_top = jnp.max(cluster_affinity, axis=1)
    row_top = lax.pmax(local_top, "cent")
    exponent = jnp.exp(cluster_affinity - row_top[:, None])
    row_total = lax.psum(jnp.sum(exponent, axis=1), "cent")
    weights = (exponent / row_total[:, None]).astype(jnp.bfloat16)
    centre_sums = lax.dot_general(
        weights, quantized, (((0,), (0,)), ((), ())), preferred_element_type=jnp.float32
    )
    counts = jnp.sum(weights.astype(jnp.float32), axis=0)
    share_rows = centre_count // lax.axis_size("dp")
    first_row = lax.axis_index("dp") * share_rows
    whole_sums, whole_counts = lax.psum((centre_sums, counts), "dp")
    part_sums = lax.dynamic_slice_in_dim(whole_sums, first_row, share_rows, 0)
    part_counts = lax.dynamic_slice_in_dim(whole_counts, first_row, share_rows, 0)
    old_rows = lax.dynamic_slice_in_dim(centroids, first_row, share_rows, 0)
    updated = (part_sums + old_rows) / (part_counts + 1.0)[:, None]
    new_centroids = updated[None]
    row_ids = boundary_rows.reshape(-1)
    owners = block_owner.reshape(-1)
    live_rows = block_live.reshape(-1)
    block_count = owners.shape[0]
    block_len = row_ids.shape[0] // block_count
    queries = jnp.take(quantized, row_ids, axis=0).reshape(block_count, block_len, width)
    keep_mask = jnp.arange(block_len, dtype=jnp.int32)[None, :] < live_rows[:, None]
    head_picks = head_index.reshape(-1)
    head_rows = jnp.take(centre_q, head_picks, axis=0)
    leading_length_power = jnp.take(centre_length_power, head_picks, axis=0)
    owner_count = lax.axis_size("cent")
    block_ids = jnp.arange(block_count, dtype=jnp.int32)
    earlier = (owners[None, :] == owners[:, None]) & (block_ids[None, :] < block_ids[:, None])
    slot_of = jnp.sum(earlier.astype(jnp.int32), axis=1)
    parcel = (
        jnp.zeros((owner_count, MOSTB, block_len, width), jnp.bfloat16)
        .at[owners, slot_of]
        .set(queries)
    )
    parcel = parcel.reshape(owner_count, MOSTB * block_len, width)
    arrived = lax.all_to_all(parcel, "cent", split_axis=0, concat_axis=0, tiled=True)
    senders = arrived.shape[0]
    slot_count = arrived.shape[1]
    residual = match_rows(
        arrived.reshape(senders * slot_count, width), head_rows, leading_length_power
    )
    returned = lax.all_to_all(
        residual.reshape(senders, slot_count, width),
        "cent",
        split_axis=0,
        concat_axis=0,
        tiled=True,
    )
    back = returned.reshape(owner_count, MOSTB, block_len, width)[owners, slot_of]
    second = jnp.where(keep_mask[:, :, None], back, jnp.zeros_like(back))
    second_resid = second.reshape(1, 1, block_count * block_len, width)
    return (new_centroids, second_resid)


def solution(mesh):
    in_specs = (
        P("dp", None),
        P("cent", None),
        P("cent", None),
        P("dp", "cent", None),
        P("dp", "cent", None),
        P("dp", "cent", None),
    )
    out_specs = (P("cent", "dp", None), P("dp", "cent", None, None))
    return jax.shard_map(
        per_device, mesh=mesh, in_specs=in_specs, out_specs=out_specs, check_vma=False
    )
```

profile of v0, /device:TPU:0, one launch (start us, length us, event | category | flops | bytes accessed | tf_op | source)
XLA Modules:
  0.0 731.3 jit_solution(666518557294251229)
XLA Ops:
  7.2 0.0 all-reduce.2.cloned.1.call-start
  7.2 3.1 convert_element_type.33
  10.3 0.0 copy-start
  10.3 4.2 convert_element_type.34
  14.5 1.3 multiply_reduce_fusion
  15.8 10.1 %fusion.1 = (f32[2048]{0:T(1024)S(1)}, f32[2048,2048]{0,1:T(8,128)}) fusion(f32[2048]{0:T(1024)S(1)} %get-tuple-element.11, f32[2048]{0:T(1024)S(1)} %get-tuple-element.12, bf16[2048,768]{1,0:T(8,128)(2,1)S(1)} %convert_element_type.33, bf16[2048,768]{1,0:T(8,128)(2,1)S(1)} %convert_element_type.34), kind=kOutput, calls=%fused_computation.10 | convolution fusion | flops 6463420416 | bytes 23093248 | tf_op jit(solution)/shard_map/dot_general | solution.py:37
  26.0 0.0 copy-done
  26.0 5.0 pmax.7
  31.0 8.5 %fusion = f32[2048]{0:T(1024)S(1)} fusion(f32[2048,2048]{0,1:T(8,128)} %get-tuple-element.8, f32[2048]{0:T(1024)S(1)} %pmax.7, f32[2048]{0:T(1024)S(1)} %get-tuple-element.11, f32[2048]{0:T(1024)S(1)} %get-tuple-element.12), kind=kLoop, calls=%fused_computation.9 | loop fusion | flops 25163776 | bytes 16809984 | tf_op jit(solution)/shard_map/reduce_sum | solution.py:46
  39.4 5.0 psum.21
  44.5 0.0 copy-start.1
  44.5 9.3 %convert_reduce_fusion = (f32[2048]{0:T(1024)S(1)}, bf16[2048,2048]{0,1:T(8,128)(2,1)S(1)}) fusion(f32[2048]{0:T(1024)S(1)} %psum.21, f32[2048]{0:T(1024)S(1)} %pmax.7, f32[2048]{0:T(1024)S(1)} %get-tuple-element.11, f32[2048]{0:T(1024)S(1)} %get-tuple-element.12, f32[2048,2048]{0,1:T(8,128)} %get-tuple-element.8), kind=kLoop, calls=%fused_computation.5 | loop fusion | flops 37746688 | bytes 25206784 | tf_op jit(solution)/shard_map/reduce_sum | solution.py:51
  53.8 0.0 copy-done.1
  53.8 0.0 copy-start.3
  53.8 0.0 copy-start.4
  53.8 8.5 %fusion.16 = f32[2048,768]{1,0:T(8,128)} fusion(bf16[2048,2048]{0,1:T(8,128)(2,1)S(1)} %get-tuple-element.6, bf16[2048,768]{1,0:T(8,128)(2,1)S(1)} %copy-done.1), kind=kOutput, calls=%fused_computation.54 | convolution fusion | flops 6442450944 | bytes 17825792 | tf_op jit(solution)/shard_map/dot_general | solution.py:48
  62.3 0.0 copy-start.2
  62.3 0.0 all-reduce.2.cloned.1.call-update
  62.3 0.0 copy-done.3
  62.3 5.4 gather_fusion.2
  67.7 0.0 copy-start.5
  67.7 0.0 copy-done.4
  67.7 0.2 convert_reduce_fusion.1
  67.9 2.2 broadcast_select_fusion.1
  70.1 0.9 broadcast_in_dim.28
  71.1 3.0 scatter_fusion
  74.0 4.5 all-to-all-start
  78.6 0.0 copy-done.2
  78.6 3.1 gather_fusion
  81.8 2.7 gather_fusion.3
  84.5 5.4 all-to-all-done
  89.9 1.4 multiply_reduce_fusion.2
  91.3 2.0 fusion.15
  93.3 0.2 fusion.5
  93.5 3.0 subtract_convert_fusion
  96.5 3.5 all-to-all-start.1
  100.0 170.1 %psum.23 = f32[2048]{0:T(1024)S(1)} all-reduce(f32[2048]{0:T(1024)S(1)} %get-tuple-element.5), channel_id=1, replica_groups=mesh['dp'=64,'cent'=2] {'dp'}, use_global_device_ids=true, to_apply=%region_8.0 | all-reduce | flops 2048 | bytes 16384 | tf_op jit(solution)/shard_map/psum | solution.py:54
  270.1 0.1 dynamic-slice_add_fusion
  270.2 0.0 copy-done.5
  270.2 0.1 fusion.8
  270.3 0.0 all-to-all-done.1
  270.3 0.6 gather_fusion.1
  270.9 1.0 broadcast_select_fusion.2
  271.9 450.9 %all-reduce.2.cloned.1.call-done = f32[2048,768]{1,0:T(8,128)} async-done(((f32[2048,768]{1,0:T(8,128)}), f32[2048,768]{1,0:T(8,128)}) %all-reduce.2.cloned.1.call-update) | async-done | bytes 6291472 | tf_op jit(solution)/shard_map/psum | solution.py:54
  722.8 1.7 divide_bitcast_fusion
  (11 shorter events, 0.1 us)
Async XLA Ops:
  7.2 715.6 %all-reduce.2.cloned.1.call-start = ((), (), s32[]{:S(2)}) async-start(), calls=%async_computation.2 | async-start | bytes 12582912 | tf_op jit(solution)/shard_map/psum | solution.py:54
  10.3 15.7 %copy-start = (bf16[2048,768]{1,0:T(8,128)(2,1)}, bf16[2048,768]{1,0:T(8,128)(2,1)S(1)}, u32[]{:S(2)}) copy-start(bf16[2048,768]{1,0:T(8,128)(2,1)S(1)} %convert_element_type.33) | copy-start | bytes 9437188
  44.5 9.3 %copy-start.1 = (bf16[2048,768]{1,0:T(8,128)(2,1)S(1)}, bf16[2048,768]{1,0:T(8,128)(2,1)}, u32[]{:S(2)}) copy-start(bf16[2048,768]{1,0:T(8,128)(2,1)} %copy-done) | copy-start | bytes 9437188
  53.8 8.5 %copy-start.3 = (s32[1,1,512]{2,1,0:T(1,128)S(1)}, s32[1,1,512]{2,1,0:T(1,128)}, u32[]{:S(2)}) copy-start(s32[1,1,512]{2,1,0:T(1,128)} %param.11) | copy-start | bytes 6148
  53.8 13.9 %copy-start.4 = (s32[1,1,4]{2,1,0:T(1,128)S(1)}, s32[1,1,4]{2,1,0:T(1,128)}, u32[]{:S(2)}) copy-start(s32[1,1,4]{2,1,0:T(1,128)} %param.12) | copy-start | bytes 52
  62.3 16.3 %copy-start.2 = (s32[1,512]{1,0:T(1,128)S(1)}, s32[1,512]{1,0:T(1,128)}, u32[]{:S(2)}) copy-start(s32[1,512]{1,0:T(1,128)} %param.10) | copy-start | bytes 6148
  67.7 202.5 %copy-start.5 = (s32[1,1,4]{2,1,0:T(1,128)S(1)}, s32[1,1,4]{2,1,0:T(1,128)}, u32[]{:S(2)}) copy-start(s32[1,1,4]{2,1,0:T(1,128)} %param.13) | copy-start | bytes 52
  74.0 15.9 %all-to-all-start = ((bf16[2,256,768]{2,1,0:T(8,128)(2,1)}), bf16[2,256,768]{2,1,0:T(8,128)(2,1)}, u32[]{:S(2)}, u32[]{:S(2)}) async-start(bf16[2,256,768]{2,1,0:T(8,128)(2,1)} %bitcast.43), calls=%async_computation | async-start | bytes 1572864 | tf_op jit(solution)/shard_map/all_to_all | solution.py:80
  96.5 173.8 %all-to-all-start.1 = ((bf16[2,256,768]{2,1,0:T(8,128)(2,1)}), bf16[2,256,768]{2,1,0:T(8,128)(2,1)S(1)}, u32[]{:S(2)}, u32[]{:S(2)}) async-start(bf16[2,256,768]{2,1,0:T(8,128)(2,1)} %bitcast.16), calls=%async_computation.1 | async-start | bytes 1572864 | tf_op jit(solution)/shard_map/all_to_all | solution.py:86
Sparse Core Ops, SparseCore 0:
  62.4 660.3 all-reduce.1
where the time goes:
time: 733 us; the launch traced here: 731 us
  waiting for transfers between devices  456 us (62%)
  blocking collectives  180 us (25%)
  other arithmetic  33.2 us (5%)
  matrix products  23.6 us (3%)
  local copies, waits for them, and re-layouts  15.7 us (2%)
  between operations  14.2 us (2%)
  starting transfers between devices  8.09 us (1%)
    psum x1, waiting for transfers between devices, per_device(): whole_sums, whole_counts = lax.psum((centre_sums, counts), 'dp')  451 us
    psum x1, blocking collectives, per_device(): whole_sums, whole_counts = lax.psum((centre_sums, counts), 'dp')  170 us
  transfers between devices with their start and end apart: 3, of which 2 were waited for; matrix products, arithmetic and copies ran while one was open for 4% of the time, Pallas kernels for 0%

commit v1 on v0

v1 whole, which is shorter than its diff:
```python
import math

import jax
import jax.numpy as jnp
from jax import lax
from jax.experimental import pallas as pl
from jax.experimental.pallas import tpu as pltpu
from jax.sharding import PartitionSpec as P

MESH = pl.DeviceIdType.MESH
F32 = jnp.float32
BF16 = jnp.bfloat16

D = 768
TILE = 256
NT = 8
NJ = 8
HALF = 128
ROWS = NJ * TILE
HEADS = 512

C1 = 0.1 * math.log2(math.e)
C2 = 0.05 * math.log2(math.e)

STAT = 0
HEAD = 2
TWIN = 4
RING = 8
CNT_T = 14
CNT_P = 15
CNT_S = 18
CNT_X = 21
SEC = 22
XHI = 28
N_REMOTE = 29

L_CEN = 0
L_VEC = 8
L_OLD = 16
L_NEW = 17
L_RES = 18
N_LOCAL = 22


def nt_dot(a, b):
    return lax.dot_general(a, b, (((1,), (1,)), ((), ())), preferred_element_type=F32)


def nn_dot(a, b):
    return jnp.dot(a, b, preferred_element_type=F32)


def kernel(
    vec, cen, hidx, brow, bown, blive,
    newc, resid,
    cst, qst, cb, qb, bias, s0, s1, e, cfin, alpha, w0, w1, cnt,
    own, tsend, trecv, rsend, rrecv, acc, xsend, xrecv, xlast,
    cs1, cs2, cs3, cr1, cr2, cr3, cr4,
    ssend, srecv, pick, hb, qs, rb, ob, old, nbuf,
    ssem, rsem, lsem,
):
    dp = lax.axis_index("dp")
    ce = lax.axis_index("cent")
    core = dp % 2
    xh = (dp // 2) % 2
    y = (dp // 4) % 4
    z = dp // 16
    prim = z * (1 - core) + y * core
    sec = y * (1 - core) + z * core
    pst = 16 * (1 - core) + 4 * core
    sst = 4 * (1 - core) + 16 * core

    def pdev(k):
        return (dp + ((prim + k) % 4 - prim) * pst, ce)

    def sdev(k):
        return (dp + ((sec + k) % 4 - sec) * sst, ce)

    twin = (dp + 1 - 2 * core, ce)
    xdev = (dp + 2 - 4 * xh, ce)
    side1 = (dp, 1 - ce)
    side2 = (dp + 2 - 4 * xh, 1 - ce)

    barrier = pltpu.get_barrier_semaphore()
    peers = [pdev(1), pdev(2), pdev(3), sdev(1), sdev(2), sdev(3), twin, xdev, side1, side2]
    for peer in peers:
        pl.semaphore_signal(barrier, inc=1, device_id=peer, device_id_type=MESH)

    def rcopy(i, src, dst, dev):
        return pltpu.make_async_remote_copy(
            src_ref=src, dst_ref=dst, send_sem=ssem.at[i], recv_sem=rsem.at[i],
            device_id=dev, device_id_type=MESH,
        )

    def lcopy(i, src, dst):
        return pltpu.make_async_copy(src, dst, lsem.at[i])

    cen_copies = [lcopy(L_CEN + t, cen.at[t, :, :, 0], cst.at[t]) for t in range(4)]
    cen_copies += [lcopy(L_CEN + 4 + t, cen.at[:, t, :, 1], cst.at[4 + t]) for t in range(4)]
    vec_copies = [
        lcopy(L_VEC + j, vec.at[pl.ds(j * TILE, TILE)], qst.at[j]) for j in range(NJ)
    ]
    vec_copies[0].start()
    for t in range(NT):
        cen_copies[t].start()
    for j in range(1, NJ):
        vec_copies[j].start()
    old_copy = lcopy(L_OLD, cen.at[z, y, xh, core], old)
    old_copy.start()

    def load_q(j):
        lcopy(L_VEC + j, vec.at[pl.ds(j * TILE, TILE)], qst.at[j]).wait()
        qb[pl.ds(pl.multiple_of(j * TILE, TILE), TILE), :] = qst[j].astype(BF16)

    def load_c(t):
        cen_copies[t].wait()
        x = cst[t].reshape(TILE, D).astype(BF16)
        cb[t] = x
        xf = x.astype(F32)
        norm = jnp.sum(xf * xf, axis=1, keepdims=True) * C2
        bias[t] = jnp.broadcast_to(norm, (TILE, TILE))

    def score(t, qj, s_ref, top):
        s = nt_dot(cb[t], qj) * C1 - bias[t]
        s_ref[t] = s
        return jnp.maximum(top, jnp.max(s.reshape(TILE // 8, 8, TILE), axis=0))

    def expo(t, j, s_ref, top, total):
        p = jnp.exp2(s_ref[t].reshape(TILE // 8, 8, TILE) - top[None])
        e[t, :, pl.ds(pl.multiple_of(j * TILE, TILE), TILE)] = p.reshape(TILE, TILE).astype(BF16)
        return total + jnp.sum(p, axis=0)

    low = jnp.full((8, TILE), -jnp.inf, F32)
    zero = jnp.zeros((8, TILE), F32)

    def whole_max(x):
        return jnp.broadcast_to(jnp.max(x, axis=0, keepdims=True), x.shape)

    def whole_sum(x):
        return jnp.broadcast_to(jnp.sum(x, axis=0, keepdims=True), x.shape)

    def q_block(j):
        return qb[pl.ds(pl.multiple_of(j * TILE, TILE), TILE), :]

    load_q(0)
    top = low
    for t in range(NT):
        load_c(t)
        top = score(t, q_block(0), s0, top)
    top = whole_max(top)

    def both(j, s_next, s_prev, top):
        load_q(j)

        def body(t, carry):
            new_top, total = carry
            new_top = score(t, q_block(j), s_next, new_top)
            total = expo(t, j - 1, s_prev, top, total)
            return new_top, total

        new_top, total = lax.fori_loop(0, NT, body, (low, zero))
        ssend[j - 1, 0] = top
        ssend[j - 1, 1] = whole_sum(total)
        return whole_max(new_top)

    def pair(i, top):
        j = 2 * i + 1
        top = both(j, s1, s0, top)
        return both(j + 1, s0, s1, top)

    top = lax.fori_loop(0, 3, pair, top)
    top = both(7, s1, s0, top)

    pl.semaphore_wait(barrier, len(peers))
    stat1 = rcopy(STAT, ssend.at[pl.ds(0, 7)], srecv.at[pl.ds(0, 7)], side1)
    stat1.start()
    total = lax.fori_loop(0, NT, lambda t, total: expo(t, 7, s1, top, total), zero)
    ssend[7, 0] = top
    ssend[7, 1] = whole_sum(total)
    stat2 = rcopy(STAT + 1, ssend.at[pl.ds(7, 1)], srecv.at[pl.ds(7, 1)], side1)
    stat2.start()

    lane = lax.broadcasted_iota(jnp.int32, (HALF, HALF), 1)

    def unit_rows(ids, place):
        column = jnp.broadcast_to(ids.astype(F32), (HALF, HALF)).T
        for k in range(ROWS // HALF):
            yield column, k

    def pick_rows(ids, place, stored_id):
        for column, k in unit_rows(ids, place):
            hit = jnp.where(column == stored_id(k).astype(F32), 1.0, 0.0)
            pick[pl.ds(place * HALF, HALF), pl.ds(k * HALF, HALF)] = hit.astype(BF16)

    def centre_id(k):
        tile, part = k // 2, k % 2
        outer = part * 2 + lane // 64
        inner = lane % 64
        inner = (inner // 32) * 64 + inner % 32
        if tile < 4:
            return tile * 512 + outer * 128 + inner
        return outer * 512 + (tile - 4) * 128 + 32 + inner

    for place in range(4):
        pick_rows(hidx[:, pl.ds(place * HALF, HALF)], place, centre_id)
    heads = nn_dot(pick[...], cb[...].reshape(ROWS, D))
    hb[ce] = heads.astype(BF16)
    head1 = rcopy(HEAD, hb.at[ce, pl.ds(0, 256)], hb.at[ce, pl.ds(0, 256)], side1)
    head2 = rcopy(HEAD + 1, hb.at[ce, pl.ds(256, 256)], hb.at[ce, pl.ds(256, 256)], side2)
    head1.start()
    head2.start()

    stat1.wait_recv()
    stat2.wait_recv()
    for j in range(NJ):
        m1, l1, m2, l2 = ssend[j, 0], ssend[j, 1], srecv[j, 0], srecv[j, 1]
        m = jnp.maximum(m1, m2)
        f1 = jnp.exp2(m1 - m)
        alpha[:, pl.ds(j * TILE, TILE)] = f1 / (l1 * f1 + l2 * jnp.exp2(m2 - m))

    def parts(base, place, step):
        if step == 0:
            t = base + (place + 2) % 4
            return (t, 0), (t, 1)
        if step == 1:
            return (base + (place + 1) % 4, 1), (base + (place + 3) % 4, 0)
        if step == 2:
            return (base + (place + 1) % 4, 0), (base + (place + 3) % 4, 1)
        return (base + place, 0), (base + place, 1)

    def tile_of(who, step):
        if who == 0:
            return parts((1 - core) * 4, sec, step)
        return parts(core * 4, prim, step)

    def scale(who, step, w_ref):
        for side, (t, half) in enumerate(tile_of(who, step)):
            count = jnp.zeros((HALF, HALF), F32)
            for c in range(NJ):
                x = e[t, pl.ds(half * HALF, HALF), pl.ds(c * TILE, TILE)].astype(F32)
                x = x.reshape(HALF // 8, 8, TILE) * alpha[:, pl.ds(c * TILE, TILE)][None]
                x = x.reshape(HALF, TILE)
                w_ref[pl.ds(side * HALF, HALF), pl.ds(c * TILE, TILE)] = x.astype(BF16)
                count = count + x[:, :HALF] + x[:, HALF:]
            cnt[pl.ds(t * 2 + half, 1), :] = jnp.sum(count.T, axis=0, keepdims=True)

    order = [(who, step) for step in range(4) for who in range(2)]
    w_refs = (w0, w1)
    twins = [rcopy(TWIN + s, tsend.at[s], trecv.at[s], twin) for s in range(4)]
    rings = [
        [rcopy(RING + 2 * s + k, rsend.at[s, k], rrecv.at[s, k], pdev((1, 3)[k])) for k in range(2)]
        for s in range(3)
    ]

    def ring_send(s):
        twins[s].wait_recv()
        for k in range(2):
            x = own[s, pl.ds(k * HALF, HALF)] + trecv[s, pl.ds(k * HALF, HALF)].astype(F32)
            if s == 2:
                rings[0][k].wait_recv()
                x = x + rrecv[0, k].astype(F32)
            rsend[s, k] = x.astype(BF16)
            rings[s][k].start()

    cnt_t = rcopy(CNT_T, cnt, cr1, twin)
    scale(0, 0, w0)
    for n, (who, step) in enumerate(order):
        out = nn_dot(w_refs[n % 2][...], qb[...])
        if n + 1 < len(order):
            scale(*order[n + 1], w_refs[(n + 1) % 2])
        if who == 0:
            tsend[step] = out.astype(BF16)
            twins[step].start()
            if step >= 1:
                ring_send(step - 1)
            if step == 3:
                cnt_t.start()
        else:
            own[step] = out

    cnt_t.wait_recv()
    cs1[...] = cnt[...] + cr1[...]
    cnt_p = [rcopy(CNT_P + k, cs1, cr2.at[k], pdev(k + 1)) for k in range(3)]
    for c in cnt_p:
        c.start()

    owner = [bown[0, b] for b in range(4)]
    slot = []
    for b in range(4):
        earlier = jnp.int32(0)
        for other in range(b):
            earlier = earlier + jnp.where(owner[other] == owner[b], 1, 0)
        slot.append(owner[b] * 2 + earlier)
    for place in range(4):
        ids = jnp.zeros((1, HALF), jnp.int32)
        for b in range(4):
            here = jnp.where(slot[b] == place, 1, 0)
            ids = ids + brow[:, pl.ds(b * HALF, HALF)] * here
        pick_rows(ids, place, lambda k: lane + k * HALF)
    qs[...] = nn_dot(pick[...], qb[...]).astype(BF16)

    twins[3].wait_recv()
    for s in (1, 2):
        for k in range(2):
            rings[s][k].wait_recv()
    for half in range(2):
        x = own[3, pl.ds(half * HALF, HALF)] + trecv[3, pl.ds(half * HALF, HALF)].astype(F32)
        x = x + rrecv[2 - half, 0].astype(F32) + rrecv[1 + half, 1].astype(F32)
        acc[pl.ds(half * 2, 2)] = x.reshape(2, 2, 32, D)

    secs = [
        [rcopy(SEC + 2 * m + k, xsend.at[m, k], xrecv.at[m, k], sdev((1, 3)[k])) for k in range(2)]
        for m in range(3)
    ]
    across, up, down = (sec + 2) % 4, (sec + 1) % 4, (sec + 3) % 4
    for m, k, chunk, part in ((0, 0, across, 0), (0, 1, across, 1), (1, 0, up, 1), (1, 1, down, 0)):
        xsend[m, k] = acc[chunk, part].astype(BF16)
        secs[m][k].start()

    for c in cnt_p:
        c.wait_recv()
    cs2[...] = cs1[...] + cr2[0] + cr2[1] + cr2[2]
    cnt_s = [rcopy(CNT_S + k, cs2, cr3.at[k], sdev(k + 1)) for k in range(3)]
    for c in cnt_s:
        c.start()

    def match(o):
        h = hb[o]
        hf = h.astype(F32)
        sq = hf * hf
        part = sq[:, :128]
        for c in range(1, D // 128):
            part = part + sq[:, c * 128:(c + 1) * 128]
        norm = jnp.concatenate(
            [jnp.sum(part[i * 128:(i + 1) * 128].T, axis=0, keepdims=True) for i in range(HEADS // 128)],
            axis=1,
        )
        q = qs[pl.ds(o * TILE, TILE), :]
        s = nt_dot(q, h) * C1 - norm * C2
        p = jnp.exp2(s - jnp.max(s, axis=1, keepdims=True))
        weights = (p / jnp.sum(p, axis=1, keepdims=True)).astype(BF16)
        r = (q.astype(F32) - nn_dot(weights, h)).astype(BF16)
        rb[pl.ds(o * 2, 2)] = r.reshape(2, HALF, D)

    head1.wait_recv()
    head2.wait_recv()
    match(0)

    for k in range(2):
        secs[0][k].wait_recv()
        chunk, part = ((up, 0), (down, 1))[k]
        xsend[2, k] = (acc[chunk, part] + xrecv[0, k].astype(F32)).astype(BF16)
        secs[2][k].start()

    match(1)

    for m in (1, 2):
        for k in range(2):
            secs[m][k].wait_recv()
    for part in range(2):
        acc[sec, part] = (
            acc[sec, part] + xrecv[2 - part, 0].astype(F32) + xrecv[1 + part, 1].astype(F32)
        )
    xlast[0] = acc[sec, 1 - xh].astype(BF16)
    last = rcopy(XHI, xlast.at[0], xlast.at[1], xdev)
    last.start()
    for c in cnt_s:
        c.wait_recv()
    cs3[...] = cs2[...] + cr3[0] + cr3[1] + cr3[2]
    cnt_x = rcopy(CNT_X, cs3, cr4, xdev)
    cnt_x.start()

    row = lax.broadcasted_iota(jnp.int32, (HALF, D), 0)
    res_copies = []
    for b in range(4):
        x = rb[slot[b]]
        ob[b] = jnp.where(row < blive[0, b], x, jnp.zeros_like(x))
        res_copies.append(lcopy(L_RES + b, ob.at[b], resid.at[pl.ds(b * HALF, HALF)]))
        res_copies[b].start()

    old_copy.wait()
    last.wait_recv()
    cnt_x.wait_recv()
    cfin[...] = cs3[...] + cr4[...]
    place = core * 1024 + prim * 256 + sec * 64 + xh * 32
    counts = jnp.broadcast_to(cfin[pl.ds(place // HALF, 1), :], (32, HALF))
    at = lax.broadcasted_iota(jnp.int32, (32, HALF), 0) + place % HALF
    hit = lax.broadcasted_iota(jnp.int32, (32, HALF), 1) == at
    count = jnp.sum(jnp.where(hit, counts, 0.0), axis=1, keepdims=True)
    total = acc[sec, xh] + xlast[1].astype(F32) + old[...]
    nbuf[...] = total / (count + 1.0)
    new_copy = lcopy(L_NEW, nbuf, newc)
    new_copy.start()

    for c in [stat1, stat2, head1, head2, cnt_t, last, cnt_x]:
        c.wait_send()
    for c in twins + cnt_p + cnt_s:
        c.wait_send()
    for group in rings + secs:
        for c in group:
            c.wait_send()
    for c in res_copies:
        c.wait()
    new_copy.wait()


def per_device(vectors, centroids, head_index, boundary_rows, block_owner, block_live):
    any_spec = pl.BlockSpec(memory_space=pl.ANY)
    vmem = pl.BlockSpec(memory_space=pltpu.VMEM)
    smem = pl.BlockSpec(memory_space=pltpu.SMEM)
    scratch = [
        pltpu.VMEM((NT, 4, 2, 32, D), F32),
        pltpu.VMEM((NJ, TILE, D), F32),
        pltpu.VMEM((NT, TILE, D), BF16),
        pltpu.VMEM((ROWS, D), BF16),
        pltpu.VMEM((NT, TILE, TILE), F32),
        pltpu.VMEM((NT, TILE, TILE), F32),
        pltpu.VMEM((NT, TILE, TILE), F32),
        pltpu.VMEM((NT, TILE, ROWS), BF16),
        pltpu.VMEM((16, HALF), F32),
        pltpu.VMEM((8, ROWS), F32),
        pltpu.VMEM((TILE, ROWS), BF16),
        pltpu.VMEM((TILE, ROWS), BF16),
        pltpu.VMEM((16, HALF), F32),
        pltpu.VMEM((4, TILE, D), F32),
        pltpu.VMEM((4, TILE, D), BF16),
        pltpu.VMEM((4, TILE, D), BF16),
        pltpu.VMEM((3, 2, HALF, D), BF16),
        pltpu.VMEM((3, 2, HALF, D), BF16),
        pltpu.VMEM((4, 2, 32, D), F32),
        pltpu.VMEM((3, 2, 32, D), BF16),
        pltpu.VMEM((3, 2, 32, D), BF16),
        pltpu.VMEM((2, 32, D), BF16),
        pltpu.VMEM((16, HALF), F32),
        pltpu.VMEM((16, HALF), F32),
        pltpu.VMEM((16, HALF), F32),
        pltpu.VMEM((16, HALF), F32),
        pltpu.VMEM((3, 16, HALF), F32),
        pltpu.VMEM((3, 16, HALF), F32),
        pltpu.VMEM((16, HALF), F32),
        pltpu.VMEM((NJ, 2, 8, TILE), F32),
        pltpu.VMEM((NJ, 2, 8, TILE), F32),
        pltpu.VMEM((HEADS, ROWS), BF16),
        pltpu.VMEM((2, HEADS, D), BF16),
        pltpu.VMEM((HEADS, D), BF16),
        pltpu.VMEM((4, HALF, D), BF16),
        pltpu.VMEM((4, HALF, D), BF16),
        pltpu.VMEM((32, D), F32),
        pltpu.VMEM((32, D), F32),
        pltpu.SemaphoreType.DMA((N_REMOTE,)),
        pltpu.SemaphoreType.DMA((N_REMOTE,)),
        pltpu.SemaphoreType.DMA((N_LOCAL,)),
    ]
    new, resid = pl.pallas_call(
        kernel,
        out_shape=(
            jax.ShapeDtypeStruct((32, D), F32),
            jax.ShapeDtypeStruct((HEADS, D), BF16),
        ),
        in_specs=[any_spec, any_spec, vmem, vmem, smem, smem],
        out_specs=(any_spec, any_spec),
        scratch_shapes=scratch,
        compiler_params=pltpu.CompilerParams(
            collective_id=0, has_side_effects=True, vmem_limit_bytes=60 * 1024 * 1024
        ),
    )(
        vectors,
        centroids.reshape(4, 4, 2, 2, 32, D),
        head_index,
        boundary_rows.reshape(1, HEADS),
        block_owner.reshape(1, 4),
        block_live.reshape(1, 4),
    )
    return new[None], resid[None, None]


def solution(mesh):
    in_specs = (
        P("dp", None),
        P("cent", None),
        P("cent", None),
        P("dp", "cent", None),
        P("dp", "cent", None),
        P("dp", "cent", None),
    )
    out_specs = (P("cent", "dp", None), P("dp", "cent", None, None))
    return jax.shard_map(
        per_device, mesh=mesh, in_specs=in_specs, out_specs=out_specs, check_vma=False
    )
```

time: 733 us -> 62.4 us (0.09)
  waiting for transfers between devices: 456 us -> 0 us
  blocking collectives: 180 us -> 0 us
  Pallas kernels: 0 us -> 57.9 us
  other arithmetic: 33.2 us -> 0 us
  matrix products: 23.6 us -> 0 us
  between operations: 14.2 us -> 0.64 us
  local copies, waits for them, and re-layouts: 15.7 us -> 3.6 us
  starting transfers between devices: 8.09 us -> 0 us
    psum x1 -> x0, waiting for transfers between devices: 451 us -> none  [per_device(): whole_sums, whole_counts = lax.psum((centre_sums, counts), 'dp')]
    psum x2 -> x0, blocking collectives: 175 us -> none  [the longest x1 170 us: per_device(): whole_sums, whole_counts = lax.psum((centre_sums, counts), 'dp')]
    pallas_call x0 -> x1, Pallas kernels: none -> 57.9 us  [per_device(): pl.pallas_call(kernel, out_shape=(jax.ShapeDtypeStruct((32, D), F32), jax...]
    dot_general x4 -> x0, matrix products: 23.6 us -> none  [the longest x1 10.1 us: per_device(): lax.dot_general(quantized, centre_q, (((1,), (1,)), ((), ())), preferred_...]
    reduce_sum x6 -> x0, other arithmetic: 20.8 us -> none  [the longest x1 9.3 us: per_device(): counts = jnp.sum(weights.astype(jnp.float32), axis=0)]
    gather x4 -> x0, local copies, waits for them, and re-layouts: 11.8 us -> none  [the longest x1 5.37 us: per_device(): jnp.take(quantized, row_ids, axis=0).reshape(block_count, block_len, width)]
    all_to_all x2 -> x0, starting transfers between devices: 8.05 us -> none  [the longest x1 4.52 us: per_device(): lax.all_to_all(parcel, 'cent', split_axis=0, concat_axis=0, tiled=True)]
  transfers between devices with their start and end apart: 3 -> 0, of which waited for: 2 -> 0; matrix products, arithmetic and copies ran while one was open for 4% -> 0% of each run, Pallas kernels for 0% -> 0%
where the time goes in v1:
time: 62.4 us; the launch traced here: 62.2 us
  Pallas kernels  57.9 us (93%)
  local copies, waits for them, and re-layouts  3.6 us (6%)
  between operations  0.64 us (1%)
    pallas_call x1, Pallas kernels, per_device(): pl.pallas_call(kernel, out_shape=(jax.ShapeDtypeStruct((32, D), F32), jax...  57.9 us
    unnamed x2, local copies, waits for them, and re-layouts  3.6 us

profile of v1, /device:TPU:0, one launch (start us, length us, event | category | flops | bytes accessed | tf_op | source)
XLA Modules:
  0.0 62.2 jit_solution(8705304064818137531)
XLA Ops:
  0.6 57.9 %shard_map.77 = (f32[32,768]{1,0:T(8,128)}, bf16[512,768]{1,0:T(8,128)(2,1)}) custom-call(f32[2048,768]{1,0:T(8,128)} %vec.1, f32[4,4,2,2,32,768]{5,4,3,2,1,0:T(8,128)} %bitcast.6, s32[1,512]{1,0:T(1,128)} %hidx.1, s32[1,512]{1,0:T(1,128)} %bitcast.9, s32[1,4]{1,0:T(1,128)} %bitcast.10, s32[1,4]{1,0:T(1,128)} %bitcast.11), custom_call_target="tpu_custom_call" | custom-call | tf_op jit(solution)/shard_map/pallas_call | solution.py:454
  58.6 1.5 %copy.10 = f32[1,32,768]{2,1,0:T(8,128)} copy(f32[1,32,768]{2,1,0:T(8,128)} %bitcast.8) | data formatting | bytes 196608
  60.1 2.1 %copy.11 = bf16[1,1,512,768]{3,2,1,0:T(8,128)(2,1)} copy(bf16[1,1,512,768]{3,2,1,0:T(8,128)(2,1)} %bitcast.7) | data formatting | bytes 1572864

commit v2 on v1

--- a/solution.py
+++ b/solution.py
@@ -26,20 +26,19 @@
 HEAD = 2
 TWIN = 4
 RING = 8
-CNT_T = 14
-CNT_P = 15
-CNT_S = 18
-CNT_X = 21
-SEC = 22
-XHI = 28
-N_REMOTE = 29
+RING2 = 12
+CNT_T = 16
+CNT_P = 17
+CNT_S = 20
+CNT_X = 23
+SEC = 24
+XHI = 27
+N_REMOTE = 28
 
 L_CEN = 0
 L_VEC = 8
 L_OLD = 16
-L_NEW = 17
-L_RES = 18
-N_LOCAL = 22
+N_LOCAL = 17
 
 
 def nt_dot(a, b):
@@ -53,10 +52,10 @@
 def kernel(
     vec, cen, hidx, brow, bown, blive,
     newc, resid,
-    cst, qst, cb, qb, bias, s0, s1, e, cfin, alpha, w0, w1, cnt,
+    cst, qst, cb, qb, qt0, qt1, qt2, bias, s0, s1, s2, e, cfin, alpha, w0, w1, cnt,
     own, tsend, trecv, rsend, rrecv, acc, xsend, xrecv, xlast,
     cs1, cs2, cs3, cr1, cr2, cr3, cr4,
-    ssend, srecv, pick, hb, qs, rb, ob, old, nbuf,
+    ssend, srecv, pick, hb, qs, rb, old,
     ssem, rsem, lsem,
 ):
     dp = lax.axis_index("dp")
@@ -101,16 +100,19 @@
         lcopy(L_VEC + j, vec.at[pl.ds(j * TILE, TILE)], qst.at[j]) for j in range(NJ)
     ]
     vec_copies[0].start()
+    vec_copies[1].start()
     for t in range(NT):
         cen_copies[t].start()
-    for j in range(1, NJ):
+    for j in range(2, NJ):
         vec_copies[j].start()
     old_copy = lcopy(L_OLD, cen.at[z, y, xh, core], old)
     old_copy.start()
 
-    def load_q(j):
+    def load_q(j, qt_ref):
         lcopy(L_VEC + j, vec.at[pl.ds(j * TILE, TILE)], qst.at[j]).wait()
-        qb[pl.ds(pl.multiple_of(j * TILE, TILE), TILE), :] = qst[j].astype(BF16)
+        x = qst[j].astype(BF16)
+        qb[pl.ds(pl.multiple_of(j * TILE, TILE), TILE), :] = x
+        qt_ref[...] = x.T
 
     def load_c(t):
         cen_copies[t].wait()
@@ -120,8 +122,8 @@
         norm = jnp.sum(xf * xf, axis=1, keepdims=True) * C2
         bias[t] = jnp.broadcast_to(norm, (TILE, TILE))
 
-    def score(t, qj, s_ref, top):
-        s = nt_dot(cb[t], qj) * C1 - bias[t]
+    def score(t, qt_ref, s_ref, top):
+        s = nn_dot(cb[t], qt_ref[...]) * C1 - bias[t]
         s_ref[t] = s
         return jnp.maximum(top, jnp.max(s.reshape(TILE // 8, 8, TILE), axis=0))
 
@@ -139,44 +141,51 @@
     def whole_sum(x):
         return jnp.broadcast_to(jnp.sum(x, axis=0, keepdims=True), x.shape)
 
-    def q_block(j):
-        return qb[pl.ds(pl.multiple_of(j * TILE, TILE), TILE), :]
-
-    load_q(0)
-    top = low
+    load_q(0, qt0)
+    load_q(1, qt1)
+    load_c(0)
+    top0, top1 = low, low
     for t in range(NT):
-        load_c(t)
-        top = score(t, q_block(0), s0, top)
-    top = whole_max(top)
-
-    def both(j, s_next, s_prev, top):
-        load_q(j)
-
-        def body(t, carry):
-            new_top, total = carry
-            new_top = score(t, q_block(j), s_next, new_top)
-            total = expo(t, j - 1, s_prev, top, total)
-            return new_top, total
-
-        new_top, total = lax.fori_loop(0, NT, body, (low, zero))
-        ssend[j - 1, 0] = top
-        ssend[j - 1, 1] = whole_sum(total)
+        if t + 1 < NT:
+            load_c(t + 1)
+        top0 = score(t, qt0, s0, top0)
+        top1 = score(t, qt1, s1, top1)
+    load_q(2, qt2)
+
+    def put_stats(j, top, total):
+        ssend[j, 0] = top
+        ssend[j, 1] = whole_sum(total)
+
+    def both(j, s_next, qt, qt_next, prevs):
+        if qt_next is not None:
+            load_q(j + 1, qt_next)
+        new_top = low
+        totals = [zero] * len(prevs)
+        for t in range(NT):
+            new_top = score(t, qt, s_next, new_top)
+            totals = [expo(t, i, s_prev, top, total) for (i, s_prev, top), total in zip(prevs, totals)]
+        for (i, _, top), total in zip(prevs, totals):
+            put_stats(i, top, total)
         return whole_max(new_top)
 
+    top = both(2, s2, qt2, qt0, [(0, s0, whole_max(top0)), (1, s1, whole_max(top1))])
+
     def pair(i, top):
-        j = 2 * i + 1
-        top = both(j, s1, s0, top)
-        return both(j + 1, s0, s1, top)
-
-    top = lax.fori_loop(0, 3, pair, top)
-    top = both(7, s1, s0, top)
+        j = 2 * i + 3
+        top = both(j, s0, qt0, qt2, [(j - 1, s2, top)])
+        return both(j + 1, s2, qt2, qt0, [(j, s0, top)])
+
+    for i in range(2):
+        top = pair(i, top)
+    top = both(7, s0, qt0, None, [(6, s2, top)])
 
     pl.semaphore_wait(barrier, len(peers))
     stat1 = rcopy(STAT, ssend.at[pl.ds(0, 7)], srecv.at[pl.ds(0, 7)], side1)
     stat1.start()
-    total = lax.fori_loop(0, NT, lambda t, total: expo(t, 7, s1, top, total), zero)
-    ssend[7, 0] = top
-    ssend[7, 1] = whole_sum(total)
+    total = zero
+    for t in range(NT):
+        total = expo(t, 7, s0, top, total)
+    put_stats(7, top, total)
     stat2 = rcopy(STAT + 1, ssend.at[pl.ds(7, 1)], srecv.at[pl.ds(7, 1)], side1)
     stat2.start()
 
@@ -244,12 +253,21 @@
                 count = count + x[:, :HALF] + x[:, HALF:]
             cnt[pl.ds(t * 2 + half, 1), :] = jnp.sum(count.T, axis=0, keepdims=True)
 
-    order = [(who, step) for step in range(4) for who in range(2)]
+    order = [(0, 0), (0, 1), (1, 0), (0, 2), (1, 1), (1, 2), (0, 3), (1, 3)]
     w_refs = (w0, w1)
     twins = [rcopy(TWIN + s, tsend.at[s], trecv.at[s], twin) for s in range(4)]
     rings = [
         [rcopy(RING + 2 * s + k, rsend.at[s, k], rrecv.at[s, k], pdev((1, 3)[k])) for k in range(2)]
-        for s in range(3)
+        for s in range(2)
+    ]
+    lead = [sec % 2 + (1 - 2 * (sec % 2)) * (k * (sec // 2) + (1 - k) * (1 - sec // 2)) for k in range(2)]
+    spots = [[pl.ds(c * 64, 64) for c in (lead[k], 1 - lead[k])] for k in range(2)]
+    ring2 = [
+        [
+            rcopy(RING2 + 2 * k + n, rsend.at[2, k, spots[k][n]], rrecv.at[2, k, spots[k][n]], pdev((1, 3)[k]))
+            for n in range(2)
+        ]
+        for k in range(2)
     ]
 
     def ring_send(s):
@@ -260,7 +278,11 @@
                 rings[0][k].wait_recv()
                 x = x + rrecv[0, k].astype(F32)
             rsend[s, k] = x.astype(BF16)
-            rings[s][k].start()
+            if s < 2:
+                rings[s][k].start()
+            else:
+                ring2[k][0].start()
+                ring2[k][1].start()
 
     cnt_t = rcopy(CNT_T, cnt, cr1, twin)
     scale(0, 0, w0)
@@ -271,12 +293,13 @@
         if who == 0:
             tsend[step] = out.astype(BF16)
             twins[step].start()
-            if step >= 1:
-                ring_send(step - 1)
             if step == 3:
                 cnt_t.start()
+                ring_send(2)
         else:
             own[step] = out
+            if step < 2:
+                ring_send(step)
 
     cnt_t.wait_recv()
     cs1[...] = cnt[...] + cr1[...]
@@ -300,29 +323,30 @@
     qs[...] = nn_dot(pick[...], qb[...]).astype(BF16)
 
     twins[3].wait_recv()
-    for s in (1, 2):
-        for k in range(2):
-            rings[s][k].wait_recv()
+    rings[1][0].wait_recv()
+    rings[1][1].wait_recv()
     for half in range(2):
         x = own[3, pl.ds(half * HALF, HALF)] + trecv[3, pl.ds(half * HALF, HALF)].astype(F32)
-        x = x + rrecv[2 - half, 0].astype(F32) + rrecv[1 + half, 1].astype(F32)
-        acc[pl.ds(half * 2, 2)] = x.reshape(2, 2, 32, D)
-
-    secs = [
-        [rcopy(SEC + 2 * m + k, xsend.at[m, k], xrecv.at[m, k], sdev((1, 3)[k])) for k in range(2)]
-        for m in range(3)
-    ]
-    across, up, down = (sec + 2) % 4, (sec + 1) % 4, (sec + 3) % 4
-    for m, k, chunk, part in ((0, 0, across, 0), (0, 1, across, 1), (1, 0, up, 1), (1, 1, down, 0)):
-        xsend[m, k] = acc[chunk, part].astype(BF16)
-        secs[m][k].start()
-
-    for c in cnt_p:
-        c.wait_recv()
-    cs2[...] = cs1[...] + cr2[0] + cr2[1] + cr2[2]
+        x = x + rrecv[1, 1 - half].astype(F32)
+        acc[pl.ds(half * 2, 2)] = x.reshape(2, 64, D)
+
+    def finish_chunk(chunk):
+        return acc[chunk] + rrecv[2, chunk // 2, pl.ds((chunk % 2) * 64, 64)].astype(F32)
+
+    secs = [rcopy(SEC + k, xsend.at[k], xrecv.at[k], sdev(k + 1)) for k in range(3)]
+
+    def send_chunk(k):
+        xsend[k] = finish_chunk((sec + k + 1) % 4).astype(BF16)
+        secs[k].start()
+
+    def counts_on():
+        for c in cnt_p:
+            c.wait_recv()
+        cs2[...] = cs1[...] + cr2[0] + cr2[1] + cr2[2]
+        for c in cnt_s:
+            c.start()
+
     cnt_s = [rcopy(CNT_S + k, cs2, cr3.at[k], sdev(k + 1)) for k in range(3)]
-    for c in cnt_s:
-        c.start()
 
     def match(o):
         h = hb[o]
@@ -342,26 +366,23 @@
         r = (q.astype(F32) - nn_dot(weights, h)).astype(BF16)
         rb[pl.ds(o * 2, 2)] = r.reshape(2, HALF, D)
 
+    for k in range(2):
+        ring2[k][0].wait_recv()
+        ring2[k][1].wait_recv()
+    for k in (1, 0, 2):
+        send_chunk(k)
+    counts_on()
+
     head1.wait_recv()
     head2.wait_recv()
     match(0)
-
-    for k in range(2):
-        secs[0][k].wait_recv()
-        chunk, part = ((up, 0), (down, 1))[k]
-        xsend[2, k] = (acc[chunk, part] + xrecv[0, k].astype(F32)).astype(BF16)
-        secs[2][k].start()
-
     match(1)
 
-    for m in (1, 2):
-        for k in range(2):
-            secs[m][k].wait_recv()
-    for part in range(2):
-        acc[sec, part] = (
-            acc[sec, part] + xrecv[2 - part, 0].astype(F32) + xrecv[1 + part, 1].astype(F32)
-        )
-    xlast[0] = acc[sec, 1 - xh].astype(BF16)
+    for c in secs:
+        c.wait_recv()
+    total = finish_chunk(sec) + xrecv[0].astype(F32) + xrecv[1].astype(F32) + xrecv[2].astype(F32)
+    acc[sec] = total
+    xlast[0] = acc[sec, pl.ds((1 - xh) * 32, 32)].astype(BF16)
     last = rcopy(XHI, xlast.at[0], xlast.at[1], xdev)
     last.start()
     for c in cnt_s:
@@ -371,12 +392,9 @@
     cnt_x.start()
 
     row = lax.broadcasted_iota(jnp.int32, (HALF, D), 0)
-    res_copies = []
     for b in range(4):
         x = rb[slot[b]]
-        ob[b] = jnp.where(row < blive[0, b], x, jnp.zeros_like(x))
-        res_copies.append(lcopy(L_RES + b, ob.at[b], resid.at[pl.ds(b * HALF, HALF)]))
-        res_copies[b].start()
+        resid[pl.ds(b * HALF, HALF), :] = jnp.where(row < blive[0, b], x, jnp.zeros_like(x))
 
     old_copy.wait()
     last.wait_recv()
@@ -387,21 +405,27 @@
     at = lax.broadcasted_iota(jnp.int32, (32, HALF), 0) + place % HALF
     hit = lax.broadcasted_iota(jnp.int32, (32, HALF), 1) == at
     count = jnp.sum(jnp.where(hit, counts, 0.0), axis=1, keepdims=True)
-    total = acc[sec, xh] + xlast[1].astype(F32) + old[...]
-    nbuf[...] = total / (count + 1.0)
-    new_copy = lcopy(L_NEW, nbuf, newc)
-    new_copy.start()
+    total = acc[sec, pl.ds(xh * 32, 32)] + xlast[1].astype(F32) + old[...]
+    newc[...] = total / (count + 1.0)
 
     for c in [stat1, stat2, head1, head2, cnt_t, last, cnt_x]:
         c.wait_send()
-    for c in twins + cnt_p + cnt_s:
+    for c in twins + cnt_p + cnt_s + secs:
         c.wait_send()
-    for group in rings + secs:
+    for group in rings + ring2:
         for c in group:
             c.wait_send()
-    for c in res_copies:
+
+
+def hand_over(new, resid, new_out, resid_out, sems):
+    copies = [
+        pltpu.make_async_copy(new, new_out, sems.at[0]),
+        pltpu.make_async_copy(resid, resid_out, sems.at[1]),
+    ]
+    for c in copies:
+        c.start()
+    for c in copies:
         c.wait()
-    new_copy.wait()
 
 
 def per_device(vectors, centroids, head_index, boundary_rows, block_owner, block_live):
@@ -413,6 +437,10 @@
         pltpu.VMEM((NJ, TILE, D), F32),
         pltpu.VMEM((NT, TILE, D), BF16),
         pltpu.VMEM((ROWS, D), BF16),
+        pltpu.VMEM((D, TILE), BF16),
+        pltpu.VMEM((D, TILE), BF16),
+        pltpu.VMEM((D, TILE), BF16),
+        pltpu.VMEM((NT, TILE, TILE), F32),
         pltpu.VMEM((NT, TILE, TILE), F32),
         pltpu.VMEM((NT, TILE, TILE), F32),
         pltpu.VMEM((NT, TILE, TILE), F32),
@@ -427,9 +455,9 @@
         pltpu.VMEM((4, TILE, D), BF16),
         pltpu.VMEM((3, 2, HALF, D), BF16),
         pltpu.VMEM((3, 2, HALF, D), BF16),
-        pltpu.VMEM((4, 2, 32, D), F32),
-        pltpu.VMEM((3, 2, 32, D), BF16),
-        pltpu.VMEM((3, 2, 32, D), BF16),
+        pltpu.VMEM((4, 64, D), F32),
+        pltpu.VMEM((3, 64, D), BF16),
+        pltpu.VMEM((3, 64, D), BF16),
         pltpu.VMEM((2, 32, D), BF16),
         pltpu.VMEM((16, HALF), F32),
         pltpu.VMEM((16, HALF), F32),
@@ -444,8 +472,6 @@
         pltpu.VMEM((2, HEADS, D), BF16),
         pltpu.VMEM((HEADS, D), BF16),
         pltpu.VMEM((4, HALF, D), BF16),
-        pltpu.VMEM((4, HALF, D), BF16),
-        pltpu.VMEM((32, D), F32),
         pltpu.VMEM((32, D), F32),
         pltpu.SemaphoreType.DMA((N_REMOTE,)),
         pltpu.SemaphoreType.DMA((N_REMOTE,)),
@@ -454,11 +480,11 @@
     new, resid = pl.pallas_call(
         kernel,
         out_shape=(
-            jax.ShapeDtypeStruct((32, D), F32),
-            jax.ShapeDtypeStruct((HEADS, D), BF16),
+            pltpu.VMEM((32, D), F32),
+            pltpu.VMEM((HEADS, D), BF16),
         ),
         in_specs=[any_spec, any_spec, vmem, vmem, smem, smem],
-        out_specs=(any_spec, any_spec),
+        out_specs=(vmem, vmem),
         scratch_shapes=scratch,
         compiler_params=pltpu.CompilerParams(
             collective_id=0, has_side_effects=True, vmem_limit_bytes=60 * 1024 * 1024
@@ -471,6 +497,16 @@
         block_owner.reshape(1, 4),
         block_live.reshape(1, 4),
     )
+    new, resid = pl.pallas_call(
+        hand_over,
+        out_shape=(
+            jax.ShapeDtypeStruct((32, D), F32),
+            jax.ShapeDtypeStruct((HEADS, D), BF16),
+        ),
+        in_specs=[vmem, vmem],
+        out_specs=(any_spec, any_spec),
+        scratch_shapes=[pltpu.SemaphoreType.DMA((2,))],
+    )(new, resid)
     return new[None], resid[None, None]
 
 

time: 62.4 us -> 53.1 us (0.85)
  the two profiles are of different devices: /device:TPU:0 before, /device:TPU:96 now
where the time goes in v2:
time: 53.1 us; the launch traced here: 53 us
  Pallas kernels  50.7 us (95%)
  local copies, waits for them, and re-layouts  1.51 us (3%)
  between operations  0.81 us (2%)
    pallas_call x1, Pallas kernels, per_device(): pl.pallas_call(kernel, out_shape=(pltpu.VMEM((32, D), F32), pltpu.VMEM((H...  48.5 us
    pallas_call x1, Pallas kernels, per_device(): pl.pallas_call(hand_over, out_shape=(jax.ShapeDtypeStruct((32, D), F32),...  2.12 us
    unnamed x4, local copies, waits for them, and re-layouts  1.51 us

profile of v2, /device:TPU:96, one launch (start us, length us, event | category | flops | bytes accessed | tf_op | source)
XLA Modules:
  0.0 53.0 jit_solution(12966183020943767854)
XLA Ops:
  0.6 48.5 %shard_map.77 = (f32[32,768]{1,0:T(8,128)S(1)}, bf16[512,768]{1,0:T(8,128)(2,1)S(1)}) custom-call(f32[2048,768]{1,0:T(8,128)} %vec.1, f32[4,4,2,2,32,768]{5,4,3,2,1,0:T(8,128)} %bitcast.6, s32[1,512]{1,0:T(1,128)} %hidx.1, s32[1,512]{1,0:T(1,128)} %bitcast.7, s32[1,4]{1,0:T(1,128)} %bitcast.8, s32[1,4]{1,0:T(1,128)} %bitcast.9), custom_call_target="tpu_custom_call" | custom-call | tf_op jit(solution)/shard_map/pallas_call | solution.py:480
  49.2 0.0 copy-start
  49.2 0.9 %copy-done = bf16[512,768]{1,0:T(8,128)(2,1)} copy-done((bf16[512,768]{1,0:T(8,128)(2,1)}, bf16[512,768]{1,0:T(8,128)(2,1)S(1)}, u32[]{:S(2)}) %copy-start) | copy-done | bytes 786456
  50.1 0.0 copy-start.1
  50.1 0.6 %copy-done.1 = f32[32,768]{1,0:T(8,128)} copy-done((f32[32,768]{1,0:T(8,128)}, f32[32,768]{1,0:T(8,128)S(1)}, u32[]{:S(2)}) %copy-start.1) | copy-done | bytes 98328
  50.7 2.1 %shard_map.78 = (f32[32,768]{1,0:T(8,128)}, bf16[512,768]{1,0:T(8,128)(2,1)}) custom-call(f32[32,768]{1,0:T(8,128)} %copy-done.1, bf16[512,768]{1,0:T(8,128)(2,1)} %copy-done), custom_call_target="tpu_custom_call" | custom-call | tf_op jit(solution)/shard_map/pallas_call | solution.py:500
Async XLA Ops:
  49.2 0.9 %copy-start = (bf16[512,768]{1,0:T(8,128)(2,1)}, bf16[512,768]{1,0:T(8,128)(2,1)S(1)}, u32[]{:S(2)}) copy-start(bf16[512,768]{1,0:T(8,128)(2,1)S(1)} %get-tuple-element.7.resid) | copy-start | bytes 2359300
  50.1 0.6 %copy-start.1 = (f32[32,768]{1,0:T(8,128)}, f32[32,768]{1,0:T(8,128)S(1)}, u32[]{:S(2)}) copy-start(f32[32,768]{1,0:T(8,128)S(1)} %get-tuple-element.6.new) | copy-start | bytes 294916

commit v3 on v2

--- a/solution.py
+++ b/solution.py
@@ -15,6 +15,7 @@
 TILE = 256
 NT = 8
 NJ = 8
+AHEAD = 2
 HALF = 128
 ROWS = NJ * TILE
 HEADS = 512
@@ -30,10 +31,9 @@
 CNT_T = 16
 CNT_P = 17
 CNT_S = 20
-CNT_X = 23
-SEC = 24
-XHI = 27
-N_REMOTE = 28
+SEC = 27
+XHI = 33
+N_REMOTE = 34
 
 L_CEN = 0
 L_VEC = 8
@@ -53,8 +53,8 @@
     vec, cen, hidx, brow, bown, blive,
     newc, resid,
     cst, qst, cb, qb, qt0, qt1, qt2, bias, s0, s1, s2, e, cfin, alpha, w0, w1, cnt,
-    own, tsend, trecv, rsend, rrecv, acc, xsend, xrecv, xlast,
-    cs1, cs2, cs3, cr1, cr2, cr3, cr4,
+    tsend, trecv, rsend, rrecv, acc, xsend, xrecv, xlast,
+    cs1, cs2, cr1, cr2, cr3,
     ssend, srecv, pick, hb, qs, rb, old,
     ssem, rsem, lsem,
 ):
@@ -75,13 +75,17 @@
     def sdev(k):
         return (dp + ((sec + k) % 4 - sec) * sst, ce)
 
+    def sxdev(k):
+        return (sdev(k)[0] + 2 - 4 * xh, ce)
+
     twin = (dp + 1 - 2 * core, ce)
     xdev = (dp + 2 - 4 * xh, ce)
     side1 = (dp, 1 - ce)
     side2 = (dp + 2 - 4 * xh, 1 - ce)
 
     barrier = pltpu.get_barrier_semaphore()
-    peers = [pdev(1), pdev(2), pdev(3), sdev(1), sdev(2), sdev(3), twin, xdev, side1, side2]
+    peers = [pdev(1), pdev(2), pdev(3), sdev(1), sdev(2), sdev(3), sxdev(1), sxdev(2), sxdev(3)]
+    peers += [twin, xdev, side1, side2]
     for peer in peers:
         pl.semaphore_signal(barrier, inc=1, device_id=peer, device_id_type=MESH)
 
@@ -100,10 +104,12 @@
         lcopy(L_VEC + j, vec.at[pl.ds(j * TILE, TILE)], qst.at[j]) for j in range(NJ)
     ]
     vec_copies[0].start()
-    vec_copies[1].start()
-    for t in range(NT):
+    cen_copies[0].start()
+    for j in range(1, AHEAD):
+        vec_copies[j].start()
+    for t in range(1, NT):
         cen_copies[t].start()
-    for j in range(2, NJ):
+    for j in range(AHEAD, NJ):
         vec_copies[j].start()
     old_copy = lcopy(L_OLD, cen.at[z, y, xh, core], old)
     old_copy.start()
@@ -120,10 +126,11 @@
         cb[t] = x
         xf = x.astype(F32)
         norm = jnp.sum(xf * xf, axis=1, keepdims=True) * C2
-        bias[t] = jnp.broadcast_to(norm, (TILE, TILE))
+        bias[t] = jnp.broadcast_to(norm, (TILE, HALF))
 
     def score(t, qt_ref, s_ref, top):
-        s = nn_dot(cb[t], qt_ref[...]) * C1 - bias[t]
+        b = bias[t]
+        s = nn_dot(cb[t], qt_ref[...]) * C1 - jnp.concatenate([b, b], axis=1)
         s_ref[t] = s
         return jnp.maximum(top, jnp.max(s.reshape(TILE // 8, 8, TILE), axis=0))
 
@@ -141,29 +148,32 @@
     def whole_sum(x):
         return jnp.broadcast_to(jnp.sum(x, axis=0, keepdims=True), x.shape)
 
+    def put_stats(j, top, total):
+        ssend[j, 0] = top
+        ssend[j, 1] = whole_sum(total)
+
     load_q(0, qt0)
-    load_q(1, qt1)
     load_c(0)
     top0, top1 = low, low
     for t in range(NT):
+        if t == 0:
+            load_q(1, qt1)
+        else:
+            top1 = score(t - 1, qt1, s1, top1)
         if t + 1 < NT:
             load_c(t + 1)
         top0 = score(t, qt0, s0, top0)
-        top1 = score(t, qt1, s1, top1)
     load_q(2, qt2)
-
-    def put_stats(j, top, total):
-        ssend[j, 0] = top
-        ssend[j, 1] = whole_sum(total)
-
-    def both(j, s_next, qt, qt_next, prevs):
+    top1 = score(NT - 1, qt1, s1, top1)
+
+    def both(j, s_next, qt_ref, qt_next, prevs):
         if qt_next is not None:
             load_q(j + 1, qt_next)
         new_top = low
         totals = [zero] * len(prevs)
         for t in range(NT):
-            new_top = score(t, qt, s_next, new_top)
-            totals = [expo(t, i, s_prev, top, total) for (i, s_prev, top), total in zip(prevs, totals)]
+            new_top = score(t, qt_ref, s_next, new_top)
+            totals = [expo(t, i, ref, top, total) for (i, ref, top), total in zip(prevs, totals)]
         for (i, _, top), total in zip(prevs, totals):
             put_stats(i, top, total)
         return whole_max(new_top)
@@ -175,16 +185,16 @@
         top = both(j, s0, qt0, qt2, [(j - 1, s2, top)])
         return both(j + 1, s2, qt2, qt0, [(j, s0, top)])
 
-    for i in range(2):
-        top = pair(i, top)
+    top = lax.fori_loop(0, 2, pair, top)
     top = both(7, s0, qt0, None, [(6, s2, top)])
+    s_last = s0
 
     pl.semaphore_wait(barrier, len(peers))
     stat1 = rcopy(STAT, ssend.at[pl.ds(0, 7)], srecv.at[pl.ds(0, 7)], side1)
     stat1.start()
     total = zero
     for t in range(NT):
-        total = expo(t, 7, s0, top, total)
+        total = expo(t, 7, s_last, top, total)
     put_stats(7, top, total)
     stat2 = rcopy(STAT + 1, ssend.at[pl.ds(7, 1)], srecv.at[pl.ds(7, 1)], side1)
     stat2.start()
@@ -218,14 +228,6 @@
     head2 = rcopy(HEAD + 1, hb.at[ce, pl.ds(256, 256)], hb.at[ce, pl.ds(256, 256)], side2)
     head1.start()
     head2.start()
-
-    stat1.wait_recv()
-    stat2.wait_recv()
-    for j in range(NJ):
-        m1, l1, m2, l2 = ssend[j, 0], ssend[j, 1], srecv[j, 0], srecv[j, 1]
-        m = jnp.maximum(m1, m2)
-        f1 = jnp.exp2(m1 - m)
-        alpha[:, pl.ds(j * TILE, TILE)] = f1 / (l1 * f1 + l2 * jnp.exp2(m2 - m))
 
     def parts(base, place, step):
         if step == 0:
@@ -242,16 +244,43 @@
             return parts((1 - core) * 4, sec, step)
         return parts(core * 4, prim, step)
 
-    def scale(who, step, w_ref):
+    def scale(who, step, w_ref, columns, counts, last):
+        out = []
         for side, (t, half) in enumerate(tile_of(who, step)):
-            count = jnp.zeros((HALF, HALF), F32)
-            for c in range(NJ):
-                x = e[t, pl.ds(half * HALF, HALF), pl.ds(c * TILE, TILE)].astype(F32)
-                x = x.reshape(HALF // 8, 8, TILE) * alpha[:, pl.ds(c * TILE, TILE)][None]
+            partial = []
+            for c in columns:
+                x = e[t, pl.ds(half * HALF, HALF), pl.ds(c * TILE, TILE)]
+                x = x.reshape(HALF // 16, 16, TILE) * alpha[:, pl.ds(c * TILE, TILE)][None]
                 x = x.reshape(HALF, TILE)
-                w_ref[pl.ds(side * HALF, HALF), pl.ds(c * TILE, TILE)] = x.astype(BF16)
-                count = count + x[:, :HALF] + x[:, HALF:]
-            cnt[pl.ds(t * 2 + half, 1), :] = jnp.sum(count.T, axis=0, keepdims=True)
+                w_ref[pl.ds(side * HALF, HALF), pl.ds(c * TILE, TILE)] = x
+                partial.append(x[:, :HALF] + x[:, HALF:])
+            count = counts[side]
+            while partial:
+                some, partial = partial[:4], partial[4:]
+                while len(some) > 1:
+                    some = [some[0] + some[1]] + some[2:] if len(some) != 4 else [some[0] + some[1], some[2] + some[3]]
+                count = count + some[0].astype(F32)
+            if last:
+                cnt[pl.ds(t * 2 + half, 1), :] = jnp.sum(count.T, axis=0, keepdims=True)
+            out.append(count)
+        return out
+
+    none = [jnp.zeros((HALF, HALF), F32)] * 2
+
+    def row_scale(j):
+        m1, l1, m2, l2 = ssend[j, 0], ssend[j, 1], srecv[j, 0], srecv[j, 1]
+        m = jnp.maximum(m1, m2)
+        f1 = jnp.exp2(m1 - m)
+        a = f1 / (l1 * f1 + l2 * jnp.exp2(m2 - m))
+        alpha[:, pl.ds(j * TILE, TILE)] = jnp.concatenate([a, a], axis=0).astype(BF16)
+
+    stat1.wait_recv()
+    for j in range(NJ - 1):
+        row_scale(j)
+    first = scale(0, 0, w0, range(NJ - 1), none, False)
+    stat2.wait_recv()
+    row_scale(NJ - 1)
+    scale(0, 0, w0, [NJ - 1], first, True)
 
     order = [(0, 0), (0, 1), (1, 0), (0, 2), (1, 1), (1, 2), (0, 3), (1, 3)]
     w_refs = (w0, w1)
@@ -270,10 +299,13 @@
         for k in range(2)
     ]
 
+    def own(s, half):
+        return cst[s, pl.ds(half * 2, 2)].reshape(HALF, D)
+
     def ring_send(s):
         twins[s].wait_recv()
         for k in range(2):
-            x = own[s, pl.ds(k * HALF, HALF)] + trecv[s, pl.ds(k * HALF, HALF)].astype(F32)
+            x = own(s, k) + trecv[s, pl.ds(k * HALF, HALF)].astype(F32)
             if s == 2:
                 rings[0][k].wait_recv()
                 x = x + rrecv[0, k].astype(F32)
@@ -285,11 +317,10 @@
                 ring2[k][1].start()
 
     cnt_t = rcopy(CNT_T, cnt, cr1, twin)
-    scale(0, 0, w0)
     for n, (who, step) in enumerate(order):
         out = nn_dot(w_refs[n % 2][...], qb[...])
         if n + 1 < len(order):
-            scale(*order[n + 1], w_refs[(n + 1) % 2])
+            scale(*order[n + 1], w_refs[(n + 1) % 2], range(NJ), none, True)
         if who == 0:
             tsend[step] = out.astype(BF16)
             twins[step].start()
@@ -297,7 +328,7 @@
                 cnt_t.start()
                 ring_send(2)
         else:
-            own[step] = out
+            cst[step] = out.reshape(4, 2, 32, D)
             if step < 2:
                 ring_send(step)
 
@@ -326,18 +357,33 @@
     rings[1][0].wait_recv()
     rings[1][1].wait_recv()
     for half in range(2):
-        x = own[3, pl.ds(half * HALF, HALF)] + trecv[3, pl.ds(half * HALF, HALF)].astype(F32)
+        x = own(3, half) + trecv[3, pl.ds(half * HALF, HALF)].astype(F32)
         x = x + rrecv[1, 1 - half].astype(F32)
         acc[pl.ds(half * 2, 2)] = x.reshape(2, 64, D)
 
-    def finish_chunk(chunk):
-        return acc[chunk] + rrecv[2, chunk // 2, pl.ds((chunk % 2) * 64, 64)].astype(F32)
-
-    secs = [rcopy(SEC + k, xsend.at[k], xrecv.at[k], sdev(k + 1)) for k in range(3)]
-
-    def send_chunk(k):
-        xsend[k] = finish_chunk((sec + k + 1) % 4).astype(BF16)
-        secs[k].start()
+    def finish_rows(chunk, part):
+        got = rrecv[2, chunk // 2, pl.ds((chunk % 2) * 64 + part * 32, 32)]
+        return acc[chunk, pl.ds(part * 32, 32)] + got.astype(F32)
+
+    odd = sec % 2
+    steps = [1 + 2 * odd, 2, 3 - 2 * odd]
+    secs = [
+        [rcopy(SEC + 2 * i + n, xsend.at[i, n], xrecv.at[i, n], sdev(k)) for n in range(2)]
+        for i, k in enumerate(steps)
+    ]
+    sides = [1 - xh, xh]
+
+    def send_chunks(pairings):
+        for n in range(2):
+            for i in pairings:
+                xsend[i, n] = finish_rows((sec + steps[i]) % 4, sides[n]).astype(BF16)
+                secs[i][n].start()
+
+    def own_rows(n):
+        total = finish_rows(sec, sides[n])
+        for i in range(3):
+            total = total + xrecv[i, n].astype(F32)
+        return total
 
     def counts_on():
         for c in cnt_p:
@@ -346,7 +392,8 @@
         for c in cnt_s:
             c.start()
 
-    cnt_s = [rcopy(CNT_S + k, cs2, cr3.at[k], sdev(k + 1)) for k in range(3)]
+    group = [sdev(1), sdev(2), sdev(3), xdev, sxdev(1), sxdev(2), sxdev(3)]
+    cnt_s = [rcopy(CNT_S + k, cs2, cr3.at[k], dev) for k, dev in enumerate(group)]
 
     def match(o):
         h = hb[o]
@@ -366,30 +413,24 @@
         r = (q.astype(F32) - nn_dot(weights, h)).astype(BF16)
         rb[pl.ds(o * 2, 2)] = r.reshape(2, HALF, D)
 
-    for k in range(2):
-        ring2[k][0].wait_recv()
-        ring2[k][1].wait_recv()
-    for k in (1, 0, 2):
-        send_chunk(k)
+    ring2[0][0].wait_recv()
+    ring2[1][0].wait_recv()
+    send_chunks((1, 0))
+    ring2[0][1].wait_recv()
+    ring2[1][1].wait_recv()
+    send_chunks((2,))
     counts_on()
 
     head1.wait_recv()
     head2.wait_recv()
     match(0)
-    match(1)
-
-    for c in secs:
-        c.wait_recv()
-    total = finish_chunk(sec) + xrecv[0].astype(F32) + xrecv[1].astype(F32) + xrecv[2].astype(F32)
-    acc[sec] = total
-    xlast[0] = acc[sec, pl.ds((1 - xh) * 32, 32)].astype(BF16)
+
+    for i in range(3):
+        secs[i][0].wait_recv()
+    xlast[0] = own_rows(0).astype(BF16)
     last = rcopy(XHI, xlast.at[0], xlast.at[1], xdev)
     last.start()
-    for c in cnt_s:
-        c.wait_recv()
-    cs3[...] = cs2[...] + cr3[0] + cr3[1] + cr3[2]
-    cnt_x = rcopy(CNT_X, cs3, cr4, xdev)
-    cnt_x.start()
+    match(1)
 
     row = lax.broadcasted_iota(jnp.int32, (HALF, D), 0)
     for b in range(4):
@@ -397,23 +438,29 @@
         resid[pl.ds(b * HALF, HALF), :] = jnp.where(row < blive[0, b], x, jnp.zeros_like(x))
 
     old_copy.wait()
-    last.wait_recv()
-    cnt_x.wait_recv()
-    cfin[...] = cs3[...] + cr4[...]
+    for i in range(3):
+        secs[i][1].wait_recv()
+    for c in cnt_s:
+        c.wait_recv()
+    counts = cs2[...]
+    for k in range(7):
+        counts = counts + cr3[k]
+    cfin[...] = counts
     place = core * 1024 + prim * 256 + sec * 64 + xh * 32
     counts = jnp.broadcast_to(cfin[pl.ds(place // HALF, 1), :], (32, HALF))
     at = lax.broadcasted_iota(jnp.int32, (32, HALF), 0) + place % HALF
     hit = lax.broadcasted_iota(jnp.int32, (32, HALF), 1) == at
     count = jnp.sum(jnp.where(hit, counts, 0.0), axis=1, keepdims=True)
-    total = acc[sec, pl.ds(xh * 32, 32)] + xlast[1].astype(F32) + old[...]
-    newc[...] = total / (count + 1.0)
-
-    for c in [stat1, stat2, head1, head2, cnt_t, last, cnt_x]:
+    total = own_rows(1) + old[...]
+    last.wait_recv()
+    newc[...] = (total + xlast[1].astype(F32)) / (count + 1.0)
+
+    for c in [stat1, stat2, head1, head2, cnt_t, last]:
         c.wait_send()
-    for c in twins + cnt_p + cnt_s + secs:
+    for c in twins + cnt_p + cnt_s:
         c.wait_send()
-    for group in rings + ring2:
-        for c in group:
+    for pair in rings + ring2 + secs:
+        for c in pair:
             c.wait_send()
 
 
@@ -440,32 +487,29 @@
         pltpu.VMEM((D, TILE), BF16),
         pltpu.VMEM((D, TILE), BF16),
         pltpu.VMEM((D, TILE), BF16),
-        pltpu.VMEM((NT, TILE, TILE), F32),
+        pltpu.VMEM((NT, TILE, HALF), F32),
         pltpu.VMEM((NT, TILE, TILE), F32),
         pltpu.VMEM((NT, TILE, TILE), F32),
         pltpu.VMEM((NT, TILE, TILE), F32),
         pltpu.VMEM((NT, TILE, ROWS), BF16),
         pltpu.VMEM((16, HALF), F32),
-        pltpu.VMEM((8, ROWS), F32),
+        pltpu.VMEM((16, ROWS), BF16),
         pltpu.VMEM((TILE, ROWS), BF16),
         pltpu.VMEM((TILE, ROWS), BF16),
         pltpu.VMEM((16, HALF), F32),
-        pltpu.VMEM((4, TILE, D), F32),
         pltpu.VMEM((4, TILE, D), BF16),
         pltpu.VMEM((4, TILE, D), BF16),
         pltpu.VMEM((3, 2, HALF, D), BF16),
         pltpu.VMEM((3, 2, HALF, D), BF16),
         pltpu.VMEM((4, 64, D), F32),
-        pltpu.VMEM((3, 64, D), BF16),
-        pltpu.VMEM((3, 64, D), BF16),
+        pltpu.VMEM((3, 2, 32, D), BF16),
+        pltpu.VMEM((3, 2, 32, D), BF16),
         pltpu.VMEM((2, 32, D), BF16),
         pltpu.VMEM((16, HALF), F32),
         pltpu.VMEM((16, HALF), F32),
         pltpu.VMEM((16, HALF), F32),
-        pltpu.VMEM((16, HALF), F32),
         pltpu.VMEM((3, 16, HALF), F32),
-        pltpu.VMEM((3, 16, HALF), F32),
-        pltpu.VMEM((16, HALF), F32),
+        pltpu.VMEM((7, 16, HALF), F32),
         pltpu.VMEM((NJ, 2, 8, TILE), F32),
         pltpu.VMEM((NJ, 2, 8, TILE), F32),
         pltpu.VMEM((HEADS, ROWS), BF16),
@@ -506,6 +550,7 @@
         in_specs=[vmem, vmem],
         out_specs=(any_spec, any_spec),
         scratch_shapes=[pltpu.SemaphoreType.DMA((2,))],
+        compiler_params=pltpu.CompilerParams(vmem_limit_bytes=4 * 1024 * 1024),
     )(new, resid)
     return new[None], resid[None, None]
 

time: 53.1 us -> 47.7 us (0.90)
  the two profiles are of different devices: /device:TPU:96 before, /device:TPU:0 now
where the time goes in v3:
time: 47.7 us; the launch traced here: 47.4 us
  Pallas kernels  46.6 us (98%)
  between operations  0.8 us (2%)
    pallas_call x1, Pallas kernels, per_device(): pl.pallas_call(kernel, out_shape=(pltpu.VMEM((32, D), F32), pltpu.VMEM((H...  45.7 us

profile of v3, /device:TPU:0, one launch (start us, length us, event | category | flops | bytes accessed | tf_op | source)
XLA Modules:
  0.0 47.4 jit_solution(9195245034642416663)
XLA Ops:
  0.6 45.7 %shard_map.77 = (f32[32,768]{1,0:T(8,128)S(1)}, bf16[512,768]{1,0:T(8,128)(2,1)S(1)}) custom-call(f32[2048,768]{1,0:T(8,128)} %vec.1, f32[4,4,2,2,32,768]{5,4,3,2,1,0:T(8,128)} %bitcast.6, s32[1,512]{1,0:T(1,128)} %hidx.1, s32[1,512]{1,0:T(1,128)} %bitcast.7, s32[1,4]{1,0:T(1,128)} %bitcast.8, s32[1,4]{1,0:T(1,128)} %bitcast.9), custom_call_target="tpu_custom_call" | custom-call | tf_op jit(solution)/shard_map/pallas_call | solution.py:524
  46.3 0.9 %shard_map.78 = (f32[32,768]{1,0:T(8,128)}, bf16[512,768]{1,0:T(8,128)(2,1)}) custom-call(f32[32,768]{1,0:T(8,128)S(1)} %get-tuple-element.6.new, bf16[512,768]{1,0:T(8,128)(2,1)S(1)} %get-tuple-element.7.resid), custom_call_target="tpu_custom_call" | custom-call | tf_op jit(solution)/shard_map/pallas_call | solution.py:544

commit v4 on v3

--- a/solution.py
+++ b/solution.py
@@ -26,14 +26,15 @@
 STAT = 0
 HEAD = 2
 TWIN = 4
-RING = 8
-RING2 = 12
-CNT_T = 16
-CNT_P = 17
-CNT_S = 20
-SEC = 27
-XHI = 33
-N_REMOTE = 34
+RING0 = 8
+RING1 = 12
+RING2 = 14
+CNT_T = 18
+CNT_P = 19
+CNT_S = 22
+SEC = 29
+XHI = 35
+N_REMOTE = 36
 
 L_CEN = 0
 L_VEC = 8
@@ -285,36 +286,42 @@
     order = [(0, 0), (0, 1), (1, 0), (0, 2), (1, 1), (1, 2), (0, 3), (1, 3)]
     w_refs = (w0, w1)
     twins = [rcopy(TWIN + s, tsend.at[s], trecv.at[s], twin) for s in range(4)]
-    rings = [
-        [rcopy(RING + 2 * s + k, rsend.at[s, k], rrecv.at[s, k], pdev((1, 3)[k])) for k in range(2)]
-        for s in range(2)
-    ]
     lead = [sec % 2 + (1 - 2 * (sec % 2)) * (k * (sec // 2) + (1 - k) * (1 - sec // 2)) for k in range(2)]
-    spots = [[pl.ds(c * 64, 64) for c in (lead[k], 1 - lead[k])] for k in range(2)]
-    ring2 = [
-        [
-            rcopy(RING2 + 2 * k + n, rsend.at[2, k, spots[k][n]], rrecv.at[2, k, spots[k][n]], pdev((1, 3)[k]))
-            for n in range(2)
+    chunks = [(lead[k], 1 - lead[k]) for k in range(2)]
+    spots = [[pl.ds(pl.multiple_of(c * 64, 64), 64) for c in chunks[k]] for k in range(2)]
+    around = [pdev(1), pdev(3)]
+
+    def ring_parts(first, s):
+        return [
+            [
+                rcopy(first + 2 * k + n, rsend.at[s, k, spots[k][n]], rrecv.at[s, k, spots[k][n]], around[k])
+                for n in range(2)
+            ]
+            for k in range(2)
         ]
-        for k in range(2)
-    ]
+
+    ring0, ring2 = ring_parts(RING0, 0), ring_parts(RING2, 2)
+    ring1 = [rcopy(RING1 + k, rsend.at[1, k], rrecv.at[1, k], around[k]) for k in range(2)]
 
     def own(s, half):
         return cst[s, pl.ds(half * 2, 2)].reshape(HALF, D)
 
-    def ring_send(s):
-        twins[s].wait_recv()
+    def send_part(s, n):
         for k in range(2):
-            x = own(s, k) + trecv[s, pl.ds(k * HALF, HALF)].astype(F32)
+            c = 2 * k + chunks[k][n]
+            x = cst[s, c].reshape(64, D)
+            x = x + trecv[s, pl.ds(pl.multiple_of(c * 64, 64), 64)].astype(F32)
             if s == 2:
-                rings[0][k].wait_recv()
-                x = x + rrecv[0, k].astype(F32)
-            rsend[s, k] = x.astype(BF16)
-            if s < 2:
-                rings[s][k].start()
-            else:
-                ring2[k][0].start()
-                ring2[k][1].start()
+                ring0[k][n].wait_recv()
+                x = x + rrecv[0, k, spots[k][n]].astype(F32)
+            rsend[s, k, spots[k][n]] = x.astype(BF16)
+            (ring2 if s == 2 else ring0)[k][n].start()
+
+    def send_middle():
+        for k in range(2):
+            x = own(1, k) + trecv[1, pl.ds(k * HALF, HALF)].astype(F32)
+            rsend[1, k] = x.astype(BF16)
+            ring1[k].start()
 
     cnt_t = rcopy(CNT_T, cnt, cr1, twin)
     for n, (who, step) in enumerate(order):
@@ -326,11 +333,19 @@
             twins[step].start()
             if step == 3:
                 cnt_t.start()
-                ring_send(2)
+                twins[2].wait_recv()
+                send_part(2, 0)
         else:
             cst[step] = out.reshape(4, 2, 32, D)
-            if step < 2:
-                ring_send(step)
+            if step == 0:
+                twins[0].wait_recv()
+                send_part(0, 0)
+                send_part(0, 1)
+            if step == 1:
+                twins[1].wait_recv()
+                send_middle()
+            if step == 3:
+                send_part(2, 1)
 
     cnt_t.wait_recv()
     cs1[...] = cnt[...] + cr1[...]
@@ -354,8 +369,8 @@
     qs[...] = nn_dot(pick[...], qb[...]).astype(BF16)
 
     twins[3].wait_recv()
-    rings[1][0].wait_recv()
-    rings[1][1].wait_recv()
+    ring1[0].wait_recv()
+    ring1[1].wait_recv()
     for half in range(2):
         x = own(3, half) + trecv[3, pl.ds(half * HALF, HALF)].astype(F32)
         x = x + rrecv[1, 1 - half].astype(F32)
@@ -457,9 +472,9 @@
 
     for c in [stat1, stat2, head1, head2, cnt_t, last]:
         c.wait_send()
-    for c in twins + cnt_p + cnt_s:
+    for c in twins + cnt_p + cnt_s + ring1:
         c.wait_send()
-    for pair in rings + ring2 + secs:
+    for pair in ring0 + ring2 + secs:
         for c in pair:
             c.wait_send()
 

time: 47.7 us -> 47.7 us (level)
  no operation moved by 1% of the time
where the time goes in v4:
time: 47.7 us; the launch traced here: 47.5 us
  Pallas kernels  46.7 us (98%)
  between operations  0.8 us (2%)
    pallas_call x1, Pallas kernels, per_device(): pl.pallas_call(kernel, out_shape=(pltpu.VMEM((32, D), F32), pltpu.VMEM((H...  45.8 us

profile of v4, /device:TPU:0, one launch (start us, length us, event | category | flops | bytes accessed | tf_op | source)
XLA Modules:
  0.0 47.5 jit_solution(13428419247855093747)
XLA Ops:
  0.6 45.8 %shard_map.77 = (f32[32,768]{1,0:T(8,128)S(1)}, bf16[512,768]{1,0:T(8,128)(2,1)S(1)}) custom-call(f32[2048,768]{1,0:T(8,128)} %vec.1, f32[4,4,2,2,32,768]{5,4,3,2,1,0:T(8,128)} %bitcast.6, s32[1,512]{1,0:T(1,128)} %hidx.1, s32[1,512]{1,0:T(1,128)} %bitcast.7, s32[1,4]{1,0:T(1,128)} %bitcast.8, s32[1,4]{1,0:T(1,128)} %bitcast.9), custom_call_target="tpu_custom_call" | custom-call | tf_op jit(solution)/shard_map/pallas_call | solution.py:539
  46.5 0.9 %shard_map.78 = (f32[32,768]{1,0:T(8,128)}, bf16[512,768]{1,0:T(8,128)(2,1)}) custom-call(f32[32,768]{1,0:T(8,128)S(1)} %get-tuple-element.6.new, bf16[512,768]{1,0:T(8,128)(2,1)S(1)} %get-tuple-element.7.resid), custom_call_target="tpu_custom_call" | custom-call | tf_op jit(solution)/shard_map/pallas_call | solution.py:559

commit v5 on v4

--- a/solution.py
+++ b/solution.py
@@ -275,16 +275,20 @@
         a = f1 / (l1 * f1 + l2 * jnp.exp2(m2 - m))
         alpha[:, pl.ds(j * TILE, TILE)] = jnp.concatenate([a, a], axis=0).astype(BF16)
 
+    order = [(0, 0), (0, 1), (1, 0), (0, 2), (1, 1), (1, 2), (0, 3), (1, 3)]
+    w_refs = (w0, w1)
+
+    early = (NJ - 1) * TILE
     stat1.wait_recv()
     for j in range(NJ - 1):
         row_scale(j)
-    first = scale(0, 0, w0, range(NJ - 1), none, False)
+    counted = [scale(*order[n], w_refs[n], range(NJ - 1), none, False) for n in range(2)]
+    cst[4] = nn_dot(w0[:, pl.ds(0, early)], qb[pl.ds(0, early), :]).reshape(4, 2, 32, D)
     stat2.wait_recv()
     row_scale(NJ - 1)
-    scale(0, 0, w0, [NJ - 1], first, True)
-
-    order = [(0, 0), (0, 1), (1, 0), (0, 2), (1, 1), (1, 2), (0, 3), (1, 3)]
-    w_refs = (w0, w1)
+    for n in range(2):
+        scale(*order[n], w_refs[n], [NJ - 1], counted[n], True)
+
     twins = [rcopy(TWIN + s, tsend.at[s], trecv.at[s], twin) for s in range(4)]
     lead = [sec % 2 + (1 - 2 * (sec % 2)) * (k * (sec // 2) + (1 - k) * (1 - sec // 2)) for k in range(2)]
     chunks = [(lead[k], 1 - lead[k]) for k in range(2)]
@@ -325,8 +329,12 @@
 
     cnt_t = rcopy(CNT_T, cnt, cr1, twin)
     for n, (who, step) in enumerate(order):
-        out = nn_dot(w_refs[n % 2][...], qb[...])
-        if n + 1 < len(order):
+        if n == 0:
+            out = nn_dot(w0[:, pl.ds(early, TILE)], qb[pl.ds(early, TILE), :])
+            out = out + cst[4].reshape(TILE, D)
+        else:
+            out = nn_dot(w_refs[n % 2][...], qb[...])
+        if 0 < n < len(order) - 1:
             scale(*order[n + 1], w_refs[(n + 1) % 2], range(NJ), none, True)
         if who == 0:
             tsend[step] = out.astype(BF16)

time: 47.7 us -> 48.2 us (1.010)
  Pallas kernels: 46.7 us -> 47.3 us
    pallas_call x1, Pallas kernels: 45.8 us -> 46.4 us  [per_device(): pl.pallas_call(kernel, out_shape=(pltpu.VMEM((32, D), F32), pltpu.VMEM((H...]
where the time goes in v5:
time: 48.2 us; the launch traced here: 48.1 us
  Pallas kernels  47.3 us (98%)
  between operations  0.8 us (2%)
    pallas_call x1, Pallas kernels, per_device(): pl.pallas_call(kernel, out_shape=(pltpu.VMEM((32, D), F32), pltpu.VMEM((H...  46.4 us

profile of v5, /device:TPU:0, one launch (start us, length us, event | category | flops | bytes accessed | tf_op | source)
XLA Modules:
  0.0 48.1 jit_solution(5672467955144046447)
XLA Ops:
  0.6 46.4 %shard_map.77 = (f32[32,768]{1,0:T(8,128)S(1)}, bf16[512,768]{1,0:T(8,128)(2,1)S(1)}) custom-call(f32[2048,768]{1,0:T(8,128)} %vec.1, f32[4,4,2,2,32,768]{5,4,3,2,1,0:T(8,128)} %bitcast.6, s32[1,512]{1,0:T(1,128)} %hidx.1, s32[1,512]{1,0:T(1,128)} %bitcast.7, s32[1,4]{1,0:T(1,128)} %bitcast.8, s32[1,4]{1,0:T(1,128)} %bitcast.9), custom_call_target="tpu_custom_call" | custom-call | tf_op jit(solution)/shard_map/pallas_call | solution.py:547
  47.0 0.9 %shard_map.78 = (f32[32,768]{1,0:T(8,128)}, bf16[512,768]{1,0:T(8,128)(2,1)}) custom-call(f32[32,768]{1,0:T(8,128)S(1)} %get-tuple-element.6.new, bf16[512,768]{1,0:T(8,128)(2,1)S(1)} %get-tuple-element.7.resid), custom_call_target="tpu_custom_call" | custom-call | tf_op jit(solution)/shard_map/pallas_call | solution.py:567

commit v6 on v4

--- a/solution.py
+++ b/solution.py
@@ -186,7 +186,8 @@
         top = both(j, s0, qt0, qt2, [(j - 1, s2, top)])
         return both(j + 1, s2, qt2, qt0, [(j, s0, top)])
 
-    top = lax.fori_loop(0, 2, pair, top)
+    for i in range(2):
+        top = pair(i, top)
     top = both(7, s0, qt0, None, [(6, s2, top)])
     s_last = s0
 

time: 47.7 us -> 47.8 us (level)
  no operation moved by 1% of the time
where the time goes in v6:
time: 47.8 us; the launch traced here: 47.5 us
  Pallas kernels  46.7 us (98%)
  between operations  0.8 us (2%)
    pallas_call x1, Pallas kernels, per_device(): pl.pallas_call(kernel, out_shape=(pltpu.VMEM((32, D), F32), pltpu.VMEM((H...  45.7 us

profile of v6, /device:TPU:0, one launch (start us, length us, event | category | flops | bytes accessed | tf_op | source)
XLA Modules:
  0.0 47.5 jit_solution(6856098008941717801)
XLA Ops:
  0.6 45.7 %shard_map.77 = (f32[32,768]{1,0:T(8,128)S(1)}, bf16[512,768]{1,0:T(8,128)(2,1)S(1)}) custom-call(f32[2048,768]{1,0:T(8,128)} %vec.1, f32[4,4,2,2,32,768]{5,4,3,2,1,0:T(8,128)} %bitcast.6, s32[1,512]{1,0:T(1,128)} %hidx.1, s32[1,512]{1,0:T(1,128)} %bitcast.7, s32[1,4]{1,0:T(1,128)} %bitcast.8, s32[1,4]{1,0:T(1,128)} %bitcast.9), custom_call_target="tpu_custom_call" | custom-call | tf_op jit(solution)/shard_map/pallas_call | solution.py:540
  46.4 0.9 %shard_map.78 = (f32[32,768]{1,0:T(8,128)}, bf16[512,768]{1,0:T(8,128)(2,1)}) custom-call(f32[32,768]{1,0:T(8,128)S(1)} %get-tuple-element.6.new, bf16[512,768]{1,0:T(8,128)(2,1)S(1)} %get-tuple-element.7.resid), custom_call_target="tpu_custom_call" | custom-call | tf_op jit(solution)/shard_map/pallas_call | solution.py:560
